TPU v7x, 128 devices: a whole 4x4x4 slice. The times are simulated.
128 devices in a mesh: grp: 4 (over x_lo, core), blk: 32 (over y, z, x_hi).
Axes of the slice: x: 4 (x_hi: 2, x_lo: 2; x = x_hi * 2 + x_lo), y: 4, z: 4, core: 2. Of those that a mesh axis runs over, the one named last changes fastest.
Arguments:
- train_grads: bfloat16 [524288, 1024], P(('grp', 'blk'))
- targets: bfloat16 [16384, 1024], P(('grp', 'blk')), may hold values from -6 to 6
Outputs:
- scores: bfloat16 [524288, 384], P(('grp', 'blk'))
All inputs are finite; a program needn't handle non-finite values.
Results may differ from a plain program's by a relative error of at most 0.014.
Values may be sent and summed in bfloat16 or wider, within the bound.
A program may use at most 128 MiB of HBM per device.

v0:
```python
import jax
import jax.numpy as jnp
from jax import lax
from jax.sharding import PartitionSpec as P

VISITS = 3


def passed_along(value, axis, steps):
    count = lax.axis_size(axis)
    pairs = [(source, (source + steps) % count) for source in range(count)]
    return lax.ppermute(value, axis, pairs)


def solve_rows(factor, block):
    right = block.astype(jnp.float32)
    middle = lax.linalg.triangular_solve(
        factor, right, left_side=False, lower=True, transpose_a=True
    )
    result = lax.linalg.triangular_solve(
        factor, middle, left_side=False, lower=True, transpose_a=False
    )
    return result.astype(jnp.bfloat16)


def per_device(train_grads, targets):
    width = train_grads.shape[1]
    blocks_count = lax.axis_size("blk")
    rows_total = train_grads.shape[0] * lax.axis_size("grp") * blocks_count
    contract_rows = (((0,), (0,)), ((), ()))
    local_gram = lax.dot_general(
        train_grads, train_grads, contract_rows, preferred_element_type=jnp.float32
    )
    gram = lax.psum(local_gram, ("grp", "blk"))
    damping = 0.1 * jnp.trace(gram) / (rows_total * width)
    precond = gram / rows_total + damping * jnp.eye(width, dtype=jnp.float32)
    factor = jnp.linalg.cholesky(precond)
    current = solve_rows(factor, targets)
    visiting = [current]
    for step in range(VISITS - 1):
        current = passed_along(current, "blk", 1)
        visiting.append(current)
    stacked = jnp.concatenate(visiting, axis=0)
    products = lax.dot_general(
        train_grads, stacked, (((1,), (1,)), ((), ())), preferred_element_type=jnp.float32
    )
    return (products / jnp.sqrt(jnp.float32(width))).astype(jnp.bfloat16)


def solution(mesh):
    in_specs = (P(("grp", "blk"), None), P(("grp", "blk"), None))
    out_specs = P(("grp", "blk"), None)
    return jax.shard_map(
        per_device, mesh=mesh, in_specs=in_specs, out_specs=out_specs, check_vma=False
    )
```

profile of v0, /device:TPU:1, one launch (start us, length us, event | category | flops | bytes accessed | tf_op | source)
XLA Modules:
  0.0 571.7 jit_solution(18218469199940600515)
XLA Ops:
  6.5 15.1 %fusion.103 = f32[1024,1024]{0,1:T(8,128)} fusion(bf16[4096,1024]{1,0:T(8,128)(2,1)} %param.2), kind=kOutput, calls=%fused_computation.225 | convolution fusion | flops 8589934592 | bytes 12582912 | tf_op jit(solution)/shard_map/dot_general | solution.py:31
  22.6 156.5 %all-reduce.3.cloned.1.call-done = f32[1024,1024]{0,1:T(8,128)} async-done(((f32[1024,1024]{0,1:T(8,128)}), f32[1024,1024]{0,1:T(8,128)}) %all-reduce.3.cloned.1.call-update) | async-done | bytes 4194320 | tf_op jit(solution)/shard_map/psum | solution.py:34
  182.7 5.0 select_add_fusion
  187.7 5.5 copy.4
  199.6 11.7 %cholesky.222 = f32[128,128]{1,0:T(8,128)S(1)} custom-call(f32[128,128]{1,0:T(8,128)S(1)} %cholesky.577), custom_call_target="Cholesky" | custom-call | tf_op jit(solution)/shard_map/jit(cholesky)/cholesky | solution.py:37
  211.4 9.8 %custom-call.64 = f32[1,128,128]{1,2,0:T(8,128)S(1)} custom-call(f32[1,128,128]{2,1,0:T(8,128)S(1)} %get-tuple-element.57), custom_call_target="InvertDiagBlocksLowerTriangular" | custom-call | tf_op jit(solution)/shard_map/jit(cholesky)/cholesky | solution.py:37
  224.6 11.7 %cholesky.243 = f32[128,128]{1,0:T(8,128)S(1)} custom-call(f32[128,128]{1,0:T(8,128)S(1)} %cholesky.581), custom_call_target="Cholesky" | custom-call | tf_op jit(solution)/shard_map/jit(cholesky)/cholesky | solution.py:37
  236.6 9.8 %custom-call.65 = f32[1,128,128]{1,2,0:T(8,128)S(1)} custom-call(f32[1,128,128]{2,1,0:T(8,128)S(1)} %get-tuple-element.55), custom_call_target="InvertDiagBlocksLowerTriangular" | custom-call | tf_op jit(solution)/shard_map/jit(cholesky)/cholesky | solution.py:37
  252.0 11.7 %cholesky.466 = f32[128,128]{1,0:T(8,128)S(1)} custom-call(f32[128,128]{1,0:T(8,128)S(1)} %cholesky.586), custom_call_target="Cholesky" | custom-call | tf_op jit(solution)/shard_map/jit(cholesky)/cholesky | solution.py:37
  264.4 9.8 %custom-call.66 = f32[1,128,128]{1,2,0:T(8,128)S(1)} custom-call(f32[1,128,128]{2,1,0:T(8,128)S(1)} %get-tuple-element.53), custom_call_target="InvertDiagBlocksLowerTriangular" | custom-call | tf_op jit(solution)/shard_map/jit(cholesky)/cholesky | solution.py:37
  279.1 11.7 %cholesky.485 = f32[128,128]{1,0:T(8,128)S(1)} custom-call(f32[128,128]{1,0:T(8,128)S(1)} %cholesky.591), custom_call_target="Cholesky" | custom-call | tf_op jit(solution)/shard_map/jit(cholesky)/cholesky | solution.py:37
  291.6 9.8 %custom-call.67 = f32[1,128,128]{1,2,0:T(8,128)S(1)} custom-call(f32[1,128,128]{2,1,0:T(8,128)S(1)} %get-tuple-element.51), custom_call_target="InvertDiagBlocksLowerTriangular" | custom-call | tf_op jit(solution)/shard_map/jit(cholesky)/cholesky | solution.py:37
  305.7 11.9 %cholesky.504 = f32[128,128]{1,0:T(8,128)S(1)} custom-call(f32[128,128]{1,0:T(8,128)S(1)} %cholesky.596), custom_call_target="Cholesky" | custom-call | tf_op jit(solution)/shard_map/jit(cholesky)/cholesky | solution.py:37
  318.3 9.8 %custom-call.68 = f32[1,128,128]{1,2,0:T(8,128)S(1)} custom-call(f32[1,128,128]{2,1,0:T(8,128)S(1)} %get-tuple-element.49), custom_call_target="InvertDiagBlocksLowerTriangular" | custom-call | tf_op jit(solution)/shard_map/jit(cholesky)/cholesky | solution.py:37
  332.3 11.7 %cholesky.524 = f32[128,128]{1,0:T(8,128)S(1)} custom-call(f32[128,128]{1,0:T(8,128)S(1)} %cholesky.601), custom_call_target="Cholesky" | custom-call | tf_op jit(solution)/shard_map/jit(cholesky)/cholesky | solution.py:37
  344.8 9.8 %custom-call.69 = f32[1,128,128]{1,2,0:T(8,128)S(1)} custom-call(f32[1,128,128]{2,1,0:T(8,128)S(1)} %get-tuple-element.47), custom_call_target="InvertDiagBlocksLowerTriangular" | custom-call | tf_op jit(solution)/shard_map/jit(cholesky)/cholesky | solution.py:37
  358.5 11.7 %cholesky.544 = f32[128,128]{1,0:T(8,128)S(1)} custom-call(f32[128,128]{1,0:T(8,128)S(1)} %cholesky.606), custom_call_target="Cholesky" | custom-call | tf_op jit(solution)/shard_map/jit(cholesky)/cholesky | solution.py:37
  371.0 9.8 %custom-call.70 = f32[1,128,128]{1,2,0:T(8,128)S(1)} custom-call(f32[1,128,128]{2,1,0:T(8,128)S(1)} %get-tuple-element.45), custom_call_target="InvertDiagBlocksLowerTriangular" | custom-call | tf_op jit(solution)/shard_map/jit(cholesky)/cholesky | solution.py:37
  383.8 11.7 %cholesky.562 = f32[128,128]{1,0:T(8,128)S(1)} custom-call(f32[128,128]{1,0:T(8,128)S(1)} %convolution_subtract_fusion.16), custom_call_target="Cholesky" | custom-call | tf_op jit(solution)/shard_map/jit(cholesky)/cholesky | solution.py:37
  410.9 23.7 %while.1 = (s32[]{:T(128)}, f32[1024,1024]{0,1:T(8,128)}, s32[8,2]{0,1:T(2,128)S(1)}, f32[8,128,128]{2,1,0:T(8,128)S(1)}, s32[]{:T(128)}) while((s32[]{:T(128)}, f32[1024,1024]{0,1:T(8,128)}, s32[8,2]{0,1:T(2,128)S(1)}, f32[8,128,128]{2,1,0:T(8,128)S(1)}, s32[]{:T(128)}) %tuple.50), condition=%wide.while_cond, body=%wide.while_body.sunk | while | flops 2 | bytes 393329 | solution.py:17
  434.6 79.0 %custom-call.71 = f32[8,128,128]{1,2,0:T(8,128)S(1)} custom-call(f32[8,128,128]{2,1,0:T(8,128)S(1)} %get-tuple-element.12), custom_call_target="InvertDiagBlocksLowerTriangular" | custom-call | tf_op jit(solution)/shard_map/triangular_solve | solution.py:17
  531.4 11.4 %collective-permute-done = bf16[128,1024]{0,1:T(8,128)(2,1)S(1)} collective-permute-done((bf16[128,1024]{0,1:T(8,128)(2,1)S(1)}, bf16[128,1024]{0,1:T(8,128)(2,1)S(1)}, u32[]{:S(2)}, u32[]{:S(2)}) %collective-permute-start) | collective-permute-done | bytes 262176 | tf_op jit(solution)/shard_map/ppermute | solution.py:12
  543.0 12.0 %collective-permute-done.1 = bf16[128,1024]{0,1:T(8,128)(2,1)S(1)} collective-permute-done((bf16[128,1024]{0,1:T(8,128)(2,1)S(1)}, bf16[128,1024]{0,1:T(8,128)(2,1)S(1)}, u32[]{:S(2)}, u32[]{:S(2)}) %collective-permute-start.1) | collective-permute-done | bytes 262176 | tf_op jit(solution)/shard_map/ppermute | solution.py:12
  555.0 6.9 %fusion = bf16[4096,384]{0,1:T(8,128)(2,1)S(1)} fusion(bf16[4096,1024]{1,0:T(8,128)(2,1)} %param.2, bf16[128,1024]{0,1:T(8,128)(2,1)S(1)} %collective-permute-done.1, bf16[128,1024]{0,1:T(8,128)(2,1)S(1)} %collective-permute-done, bf16[128,1024]{0,1:T(8,128)(2,1)S(1)} %constant_dynamic-update-slice_fusion.36), kind=kOutput, calls=%fused_computation.3 | convolution fusion | flops 3226730496 | bytes 12320768 | tf_op jit(solution)/shard_map/dot_general | solution.py:44
  (166 shorter events, 97.7 us)
Async XLA Ops:
  6.5 172.6 %all-reduce.3.cloned.1.call-start = ((), (), s32[]{:S(2)}) async-start(), calls=%async_computation | async-start | bytes 8388608 | tf_op jit(solution)/shard_map/psum | solution.py:34
  21.6 0.9 copy-start.3
  197.7 1.9 copy-start.2
  247.5 2.0 copy-start
  513.6 9.0 %copy-start.1 = (f32[1024,1024]{0,1:T(8,128)S(1)}, f32[1024,1024]{0,1:T(8,128)}, u32[]{:S(2)}) copy-start(f32[1024,1024]{0,1:T(8,128)} %get-tuple-element.122) | copy-start | bytes 12582916
  529.8 13.0 %collective-permute-start = (bf16[128,1024]{0,1:T(8,128)(2,1)S(1)}, bf16[128,1024]{0,1:T(8,128)(2,1)S(1)}, u32[]{:S(2)}, u32[]{:S(2)}) collective-permute-start(bf16[128,1024]{0,1:T(8,128)(2,1)S(1)} %constant_dynamic-update-slice_fusion.36), channel_id=1, source_target_pairs={{0,1},{1,2},{2,3},{3,4},{4,5},{5,6},{6,7},{7,8},{8,9},{9,10},{10,1... | collective-permute-start | bytes 786440 | tf_op jit(solution)/shard_map/ppermute | solution.py:12
  542.8 12.2 %collective-permute-start.1 = (bf16[128,1024]{0,1:T(8,128)(2,1)S(1)}, bf16[128,1024]{0,1:T(8,128)(2,1)S(1)}, u32[]{:S(2)}, u32[]{:S(2)}) collective-permute-start(bf16[128,1024]{0,1:T(8,128)(2,1)S(1)} %collective-permute-done), channel_id=1, source_target_pairs={{0,1},{1,2},{2,3},{3,4},{4,5},{5,6},{6,7},{7,8},{8,9},{9,10},{10,1... | collective-permute-start | bytes 786440 | tf_op jit(solution)/shard_map/ppermute | solution.py:12
Sparse Core Ops, SparseCore 0:
  21.7 157.3 all-reduce.2
where the time goes:
time: 578 us; the launch traced here: 572 us
  other arithmetic  264 us (46%)
  waiting for transfers between devices  180 us (31%)
  matrix products  63.8 us (11%)
  local copies, waits for them, and re-layouts  42.3 us (7%)
  between operations  19.9 us (3%)
    another operation x30, other arithmetic, per_device(): factor = jnp.linalg.cholesky(precond)  167 us
    psum x1, waiting for transfers between devices, per_device(): gram = lax.psum(local_gram, ('grp', 'blk'))  156 us
    another operation x3, other arithmetic, solve_rows(): lax.linalg.triangular_solve(factor, right, left_side=False, lower=True, t...  83.8 us
    another operation x14, matrix products, per_device(): factor = jnp.linalg.cholesky(precond)  26.1 us
    another operation x40, local copies, waits for them, and re-layouts  23.5 us
    ppermute x2, waiting for transfers between devices, passed_along(): return lax.ppermute(value, axis, pairs)  23.4 us
    dot_general x1, matrix products, per_device(): lax.dot_general(train_grads, train_grads, contract_rows, preferred_elemen...  15.1 us
  transfers between devices with their start and end apart: 3, of which 3 were waited for; matrix products, arithmetic and copies ran while one was open for 0% of the time, Pallas kernels for 0%

commit v1 on v0

v1 whole, which is shorter than its diff:
```python
import functools

import jax
import jax.numpy as jnp
from jax import lax
from jax.experimental import pallas as pl
from jax.experimental.pallas import tpu as pltpu
from jax.sharding import PartitionSpec as P

VISITS = 3
NB = 128
TILE = 256
F32 = jnp.float32
BF16 = jnp.bfloat16


def wide(x):
    return jnp.broadcast_to(x, (8, NB))


def split2(x):
    hi = x.astype(BF16)
    return hi, (x - hi.astype(F32)).astype(BF16)


def split3(x):
    hi = x.astype(BF16)
    rest = x - hi.astype(F32)
    mid = rest.astype(BF16)
    return hi, mid, (rest - mid.astype(F32)).astype(BF16)


def dot(a, b):
    return jnp.dot(a, b, preferred_element_type=F32)


def dot3(a, b):
    ah, al = a
    bh, bl = b
    return dot(jnp.concatenate([ah, al], axis=1), jnp.concatenate([bh, bh], axis=0)) + dot(ah, bl)


PAIRS = ((0, 0), (0, 1), (1, 0), (1, 1), (0, 2), (2, 0))


def dot6(a, b):
    left = jnp.concatenate([a[p] for p, _ in PAIRS], axis=1)
    return dot(left, jnp.concatenate([b[q] for _, q in PAIRS], axis=0))


def outer6(a, b):
    a, b = split3(a), split3(b)
    left = jnp.concatenate([a[p] for p, _ in PAIRS], axis=0)
    right = jnp.concatenate([b[q] for _, q in PAIRS], axis=0)
    return lax.dot_general(left, right, (((0,), (0,)), ((), ())), preferred_element_type=F32)


def total(terms):
    while len(terms) > 1:
        terms = [terms[i] + terms[i + 1] for i in range(0, len(terms), 2)]
    return terms[0]


def pivot_rows(rows, k, buf):
    lane = lax.broadcasted_iota(jnp.int32, (8, NB), 1)
    sub = lax.broadcasted_iota(jnp.int32, (8, NB), 0)
    y = jnp.where((lane >= k) & (lane < k + 8), -(lane == sub + k).astype(F32), rows)
    for j in range(8):
        buf[j] = wide(rows[:, k + j : k + j + 1])
    m = [buf[j] for j in range(8)]
    for b in range(0, 8, 2):
        if b == 0:
            row = lambda i, j: wide(buf[j, i : i + 1, :])
        else:
            row = lambda i, j: wide(m[j][i : i + 1, :])
        e, f, g = row(b, b), row(b, b + 1), row(b + 1, b + 1)
        inv = 1.0 / (e * g - f * f)
        ie, jf, ig = g * inv, f * inv, e * inv
        left0 = jnp.where(sub == b, -1.0, jnp.where(sub == b + 1, 0.0, m[b]))
        left1 = jnp.where(sub == b + 1, -1.0, jnp.where(sub == b, 0.0, m[b + 1]))
        pair = (sub == b) | (sub == b + 1)

        def step(x, x0, x1):
            u0, u1 = ie * x0 - jf * x1, ig * x1 - jf * x0
            return jnp.where(pair, 0.0, x) - (left0 * u0 + left1 * u1)

        for j in range(b + 2, 8):
            m[j] = step(m[j], row(b, j), row(b + 1, j))
        y = step(y, wide(y[b : b + 1, :]), wide(y[b + 1 : b + 2, :]))
    return y


def neg_inverse(a, buf):
    lane = lax.broadcasted_iota(jnp.int32, (8, NB), 1)
    a = list(a)
    count = len(a)
    for g in range(count):
        k = 8 * g
        own = (lane >= k) & (lane < k + 8)
        rows = a[g]
        y = pivot_rows(rows, k, buf.at[g % 2])
        if g + 1 < count:
            t = a[g + 1]
            terms = [wide(t[:, k + j : k + j + 1]) * wide(y[j : j + 1, :]) for j in range(8)]
            a[g + 1] = jnp.where(own, 0.0, t) - total(terms)
        change = outer6(rows, y)
        for t in range(count):
            if t != g and t != g + 1:
                a[t] = jnp.where(own, 0.0, a[t]) - change[8 * t : 8 * t + 8, :]
        a[g] = y
    return a


def inverse(block, buf):
    block = 0.5 * (block + block.T)
    tiles = [block[8 * t : 8 * t + 8, :] for t in range(NB // 8)]
    return -jnp.concatenate(neg_inverse(tiles, buf), axis=0)


def solve_kernel(
    rows_total, gram_ref, right_ref, train_ref, out_ref, mat, left, buf, held, scored, x_ref, in_sem, out_sem
):
    width = gram_ref.shape[0]
    nblk = width // NB
    nrhs = right_ref.shape[0]
    rows = train_ref.shape[0]
    pieces = 8
    depth = rows // pieces
    load = pltpu.make_async_copy(train_ref, held, in_sem)
    load.start()

    eye = (lax.broadcasted_iota(jnp.int32, (NB, NB), 0) == lax.broadcasted_iota(jnp.int32, (NB, NB), 1)).astype(F32)
    diag = jnp.zeros((NB, NB), F32)
    for c in range(nblk):
        diag = diag + gram_ref[c * NB : (c + 1) * NB, c * NB : (c + 1) * NB] * eye
    trace = jnp.sum(jnp.sum(diag, axis=0, keepdims=True), axis=1, keepdims=True)
    damping = (0.1 * trace) / (rows_total * width)
    mat[:, :width] = gram_ref[...] * (1.0 / rows_total)
    for c in range(nblk):
        mat[c * NB : (c + 1) * NB, c * NB : (c + 1) * NB] += damping * eye
    for c in range(nrhs // NB):
        mat[:, width + c * NB : width + (c + 1) * NB] = right_ref[c * NB : (c + 1) * NB, :].astype(F32).T

    def step(j, _):
        here = pl.ds(pl.multiple_of(j * NB, NB), NB)
        inv = split3(inverse(mat[here, here], buf))
        inv = jnp.concatenate([inv[p] for p, _ in PAIRS], axis=1)
        hi, lo = split2(mat[:, here])
        left[:, :NB] = hi
        left[:, NB:] = lo

        def update(cols):
            row = split3(mat[here, cols])
            w = dot(inv, jnp.concatenate([row[q] for _, q in PAIRS], axis=0))
            wh, wl = split2(w)
            mat[:, cols] -= dot(left[...], jnp.concatenate([wh, wh], axis=0)) + dot(left[:, :NB], wl)
            mat[here, cols] = w

        lax.fori_loop((j + 1) // 2, width // TILE, lambda q, _: (update(pl.ds(pl.multiple_of(q * TILE, TILE), TILE)), 0)[1], 0)
        update(pl.ds(width, TILE))
        update(pl.ds(width + TILE, nrhs - TILE))
        return 0

    lax.fori_loop(0, nblk, step, 0)
    x_ref[...] = mat[:, width:].astype(BF16)
    load.wait()
    scale = 1.0 / (width ** 0.5)

    def score(p, _):
        part = pl.ds(pl.multiple_of(p * depth, depth), depth)
        scored[part, :] = (dot(held[part, :], x_ref[...]) * scale).astype(BF16)
        pltpu.make_async_copy(scored.at[part], out_ref.at[part], out_sem).start()
        return 0

    lax.fori_loop(0, pieces, score, 0)
    pltpu.make_async_copy(scored, out_ref, out_sem).wait()


def solve_and_score(gram, right, train, rows_total):
    width = gram.shape[0]
    rows = train.shape[0]
    nrhs = right.shape[0]
    return pl.pallas_call(
        functools.partial(solve_kernel, rows_total),
        out_shape=jax.ShapeDtypeStruct((rows, nrhs), BF16),
        in_specs=[
            pl.BlockSpec(memory_space=pltpu.VMEM),
            pl.BlockSpec(memory_space=pltpu.VMEM),
            pl.BlockSpec(memory_space=pl.ANY),
        ],
        out_specs=pl.BlockSpec(memory_space=pl.ANY),
        scratch_shapes=[
            pltpu.VMEM((width, width + nrhs), F32),
            pltpu.VMEM((width, 2 * NB), BF16),
            pltpu.VMEM((2, 8, 8, NB), F32),
            pltpu.VMEM((rows, width), BF16),
            pltpu.VMEM((rows, nrhs), BF16),
            pltpu.VMEM((width, nrhs), BF16),
            pltpu.SemaphoreType.DMA,
            pltpu.SemaphoreType.DMA,
        ],
        compiler_params=pltpu.CompilerParams(vmem_limit_bytes=56 << 20),
        name="solve_and_score",
    )(gram, right, train)


def passed_along(value, axis, steps):
    count = lax.axis_size(axis)
    pairs = [(source, (source + steps) % count) for source in range(count)]
    return lax.ppermute(value, axis, pairs)


def per_device(train_grads, targets):
    rows_total = train_grads.shape[0] * lax.axis_size("grp") * lax.axis_size("blk")
    visiting = [targets]
    for step in range(1, VISITS):
        visiting.append(passed_along(targets, "blk", step))
    right = jnp.concatenate(visiting, axis=0)
    local_gram = lax.dot_general(train_grads, train_grads, (((0,), (0,)), ((), ())), preferred_element_type=F32)
    gram = lax.psum(local_gram, ("grp", "blk"))
    return solve_and_score(gram, right, train_grads, rows_total)


def solution(mesh):
    spec = P(("grp", "blk"), None)
    return jax.shard_map(per_device, mesh=mesh, in_specs=(spec, spec), out_specs=spec, check_vma=False)
```

time: 578 us -> 248 us (0.43); the launches traced: 572 us -> 248 us
  other arithmetic: 264 us -> 0.98 us
  Pallas kernels: 0 us -> 60.3 us
  matrix products: 63.8 us -> 15.1 us
  local copies, waits for them, and re-layouts: 42.3 us -> 0.93 us
  waiting for transfers between devices: 180 us -> 152 us
  between operations: 19.9 us -> 13.4 us
    another operation x34 -> x0, other arithmetic: 251 us -> none  [the longest x30 167 us: per_device(): factor = jnp.linalg.cholesky(precond)]
    pallas_call x0 -> x1, Pallas kernels: none -> 60.3 us  [solve_and_score(): pl.pallas_call(functools.partial(solve_kernel, rows_total), out_shape=jax...]
    another operation x44 -> x0, matrix products: 41.8 us -> none  [the longest x14 26.1 us: per_device(): factor = jnp.linalg.cholesky(precond)]
    another operation x69 -> x0, local copies, waits for them, and re-layouts: 29.1 us -> none
    psum x1, waiting for transfers between devices: 156 us -> 133 us  [per_device(): gram = lax.psum(local_gram, ('grp', 'blk'))]
    dot_general x2 -> x1, matrix products: 22 us -> 15.1 us  [per_device(): lax.dot_general(train_grads, train_grads, (((0,), (0,)), ((), ())), prefe...]
where the time goes in v1:
time: 248 us
  waiting for transfers between devices  152 us (61%)
  Pallas kernels  60.3 us (24%)
  matrix products  15.1 us (6%)
  between operations  13.4 us (5%)
  starting transfers between devices  5.21 us (2%)
    psum x1, waiting for transfers between devices, per_device(): gram = lax.psum(local_gram, ('grp', 'blk'))  133 us
    pallas_call x1, Pallas kernels, solve_and_score(): pl.pallas_call(functools.partial(solve_kernel, rows_total), out_shape=jax...  60.3 us
    ppermute x2, waiting for transfers between devices, passed_along(): return lax.ppermute(value, axis, pairs)  18.6 us
    dot_general x1, matrix products, per_device(): lax.dot_general(train_grads, train_grads, (((0,), (0,)), ((), ())), prefe...  15.1 us
    ppermute x2, starting transfers between devices, passed_along(): return lax.ppermute(value, axis, pairs)  5.21 us
  transfers between devices with their start and end apart: 3, of which 3 were waited for; matrix products, arithmetic and copies ran while one was open for 0% of the time, Pallas kernels for 0%

profile of v1, /device:TPU:1, one launch (start us, length us, event | category | flops | bytes accessed | tf_op | source)
XLA Modules:
  0.0 247.8 jit_solution(1109473872349682550)
XLA Ops:
  6.5 0.0 all-reduce.2.cloned.1.call-start
  6.5 15.1 %fusion = f32[1024,1024]{1,0:T(8,128)} fusion(bf16[4096,1024]{1,0:T(8,128)(2,1)} %train_ref.1), kind=kOutput, calls=%fused_computation.1 | convolution fusion | flops 8589934592 | bytes 12582912 | tf_op jit(solution)/shard_map/dot_general | solution.py:219
  21.6 0.0 copy-start
  21.6 0.0 all-reduce.2.cloned.1.call-update
  21.7 0.9 copy-done
  22.6 3.6 %collective-permute-start = (bf16[128,1024]{1,0:T(8,128)(2,1)S(1)}, bf16[128,1024]{1,0:T(8,128)(2,1)S(1)}, u32[]{:S(2)}, u32[]{:S(2)}) collective-permute-start(bf16[128,1024]{1,0:T(8,128)(2,1)S(1)} %copy-done), channel_id=1, source_target_pairs={{0,1},{1,2},{2,3},{3,4},{4,5},{5,6},{6,7},{7,8},{8,9},{9,10},{10,1... | collective-permute-start | bytes 786440 | tf_op jit(solution)/shard_map/ppermute | solution.py:210
  26.2 1.6 collective-permute-start.1
  27.8 10.3 %collective-permute-done = bf16[128,1024]{1,0:T(8,128)(2,1)S(1)} collective-permute-done((bf16[128,1024]{1,0:T(8,128)(2,1)S(1)}, bf16[128,1024]{1,0:T(8,128)(2,1)S(1)}, u32[]{:S(2)}, u32[]{:S(2)}) %collective-permute-start) | collective-permute-done | bytes 262176 | tf_op jit(solution)/shard_map/ppermute | solution.py:210
  38.1 8.3 %collective-permute-done.1 = bf16[128,1024]{1,0:T(8,128)(2,1)S(1)} collective-permute-done((bf16[128,1024]{1,0:T(8,128)(2,1)S(1)}, bf16[128,1024]{1,0:T(8,128)(2,1)S(1)}, u32[]{:S(2)}, u32[]{:S(2)}) %collective-permute-start.1) | collective-permute-done | bytes 262176 | tf_op jit(solution)/shard_map/ppermute | solution.py:210
  46.4 1.0 pad_maximum_fusion.right_ref
  47.4 133.3 %all-reduce.2.cloned.1.call-done.gram_ref = f32[1024,1024]{1,0:T(8,128)} async-done(((f32[1024,1024]{1,0:T(8,128)}), f32[1024,1024]{1,0:T(8,128)}) %all-reduce.2.cloned.1.call-update) | async-done | bytes 4194320 | tf_op jit(solution)/shard_map/psum | solution.py:220
  180.7 60.3 %solve_and_score.1 = bf16[4096,384]{1,0:T(8,128)(2,1)} custom-call(f32[1024,1024]{1,0:T(8,128)} %all-reduce.2.cloned.1.call-done.gram_ref, bf16[384,1024]{1,0:T(8,128)(2,1)} %pad_maximum_fusion.right_ref, bf16[4096,1024]{1,0:T(8,128)(2,1)} %train_ref.1), custom_call_target="tpu_custom_call" | custom-call | tf_op jit(solution)/shard_map/solve_and_score/pallas_call | solution.py:183
Async XLA Ops:
  6.5 174.1 %all-reduce.2.cloned.1.call-start = ((), (), s32[]{:S(2)}) async-start(), calls=%async_computation | async-start | bytes 8388608 | tf_op jit(solution)/shard_map/psum | solution.py:220
  21.6 0.9 copy-start
  22.6 15.5 %collective-permute-start = (bf16[128,1024]{1,0:T(8,128)(2,1)S(1)}, bf16[128,1024]{1,0:T(8,128)(2,1)S(1)}, u32[]{:S(2)}, u32[]{:S(2)}) collective-permute-start(bf16[128,1024]{1,0:T(8,128)(2,1)S(1)} %copy-done), channel_id=1, source_target_pairs={{0,1},{1,2},{2,3},{3,4},{4,5},{5,6},{6,7},{7,8},{8,9},{9,10},{10,1... | collective-permute-start | bytes 786440 | tf_op jit(solution)/shard_map/ppermute | solution.py:210
  26.2 20.2 %collective-permute-start.1 = (bf16[128,1024]{1,0:T(8,128)(2,1)S(1)}, bf16[128,1024]{1,0:T(8,128)(2,1)S(1)}, u32[]{:S(2)}, u32[]{:S(2)}) collective-permute-start(bf16[128,1024]{1,0:T(8,128)(2,1)S(1)} %copy-done), channel_id=1, source_target_pairs={{0,2},{1,3},{2,4},{3,5},{4,6},{5,7},{6,8},{7,9},{8,10},{9,11},{10,... | collective-permute-start | bytes 786440 | tf_op jit(solution)/shard_map/ppermute | solution.py:210
Sparse Core Ops, SparseCore 0:
  21.8 158.8 all-reduce.1

commit v2 on v1

--- a/solution.py
+++ b/solution.py
@@ -12,6 +12,13 @@
 TILE = 256
 F32 = jnp.float32
 BF16 = jnp.bfloat16
+MESH = pl.DeviceIdType.MESH
+
+
+def upper_blocks(count):
+    first = [i for i in range(count) if i < 2 or i >= count - 2]
+    rest = [i for i in range(count) if 2 <= i < count - 2]
+    return [(i, c) for i in first + rest for c in range(i, count)]
 
 
 def wide(x):
@@ -120,7 +127,7 @@
 def solve_kernel(
     rows_total, gram_ref, right_ref, train_ref, out_ref, mat, left, buf, held, scored, x_ref, in_sem, out_sem
 ):
-    width = gram_ref.shape[0]
+    width = right_ref.shape[1]
     nblk = width // NB
     nrhs = right_ref.shape[0]
     rows = train_ref.shape[0]
@@ -130,14 +137,20 @@
     load.start()
 
     eye = (lax.broadcasted_iota(jnp.int32, (NB, NB), 0) == lax.broadcasted_iota(jnp.int32, (NB, NB), 1)).astype(F32)
+    blocks = upper_blocks(nblk)
     diag = jnp.zeros((NB, NB), F32)
-    for c in range(nblk):
-        diag = diag + gram_ref[c * NB : (c + 1) * NB, c * NB : (c + 1) * NB] * eye
+    for n, (i, c) in enumerate(blocks):
+        if i == c:
+            diag = diag + gram_ref[n * NB : (n + 1) * NB, :] * eye
     trace = jnp.sum(jnp.sum(diag, axis=0, keepdims=True), axis=1, keepdims=True)
     damping = (0.1 * trace) / (rows_total * width)
-    mat[:, :width] = gram_ref[...] * (1.0 / rows_total)
-    for c in range(nblk):
-        mat[c * NB : (c + 1) * NB, c * NB : (c + 1) * NB] += damping * eye
+    for n, (i, c) in enumerate(blocks):
+        block = gram_ref[n * NB : (n + 1) * NB, :] * (1.0 / rows_total)
+        if i == c:
+            mat[i * NB : (i + 1) * NB, i * NB : (i + 1) * NB] = block + damping * eye
+        else:
+            mat[i * NB : (i + 1) * NB, c * NB : (c + 1) * NB] = block
+            mat[c * NB : (c + 1) * NB, i * NB : (i + 1) * NB] = block.T
     for c in range(nrhs // NB):
         mat[:, width + c * NB : width + (c + 1) * NB] = right_ref[c * NB : (c + 1) * NB, :].astype(F32).T
 
@@ -177,8 +190,7 @@
 
 
 def solve_and_score(gram, right, train, rows_total):
-    width = gram.shape[0]
-    rows = train.shape[0]
+    rows, width = train.shape
     nrhs = right.shape[0]
     return pl.pallas_call(
         functools.partial(solve_kernel, rows_total),
@@ -204,20 +216,211 @@
     )(gram, right, train)
 
 
-def passed_along(value, axis, steps):
-    count = lax.axis_size(axis)
-    pairs = [(source, (source + steps) % count) for source in range(count)]
-    return lax.ppermute(value, axis, pairs)
+def gram_kernel(train_ref, out_ref, held, sems):
+    width = held.shape[1]
+    chunks = sems.shape[0]
+    depth = held.shape[0] // chunks
+    loads = [
+        pltpu.make_async_copy(train_ref.at[pl.ds(k * depth, depth)], held.at[pl.ds(k * depth, depth)], sems.at[k])
+        for k in range(chunks)
+    ]
+    for load in loads:
+        load.start()
+    place = {key: n for n, key in enumerate(upper_blocks(width // NB))}
+    for k in range(chunks):
+        loads[k].wait()
+        for first in range(0, width // NB, 2):
+            part = held[k * depth : (k + 1) * depth, first * NB :]
+            res = lax.dot_general(part[:, : 2 * NB], part, (((0,), (0,)), ((), ())), preferred_element_type=F32)
+            for i in (first, first + 1):
+                for c in range(i, width // NB):
+                    n = place[i, c]
+                    block = res[(i - first) * NB : (i - first + 1) * NB, (c - first) * NB : (c - first + 1) * NB]
+                    if k == 0:
+                        out_ref[n * NB : (n + 1) * NB, :] = block
+                    else:
+                        out_ref[n * NB : (n + 1) * NB, :] += block
+
+
+def packed_gram(train):
+    rows, width = train.shape
+    count = len(upper_blocks(width // NB))
+    return pl.pallas_call(
+        gram_kernel,
+        out_shape=jax.ShapeDtypeStruct((count * NB, NB), F32),
+        in_specs=[pl.BlockSpec(memory_space=pl.ANY)],
+        out_specs=pl.BlockSpec(memory_space=pltpu.VMEM),
+        scratch_shapes=[pltpu.VMEM((rows, width), BF16), pltpu.SemaphoreType.DMA((4,))],
+        compiler_params=pltpu.CompilerParams(vmem_limit_bytes=56 << 20),
+        name="packed_gram",
+    )(train)
+
+
+RING = 4
+PARTS = 3
+
+
+def sum_kernel(
+    gram_ref, target_ref, out_ref, right_ref, pair, work, got1, sum1, got2, sum2, got3, full2,
+    send0, recv0, send1, recv1, send2, recv2, send3, recv3, send4, recv4, send5, recv5, send6, recv6, send7, recv7, own_sem,
+):
+    grp, blk = lax.axis_index("grp"), lax.axis_index("blk")
+    core = lax.rem(grp, 2)
+    pos = (lax.rem(blk, 2) * 2 + grp // 2, blk // 8, lax.rem(blk // 2, RING))
+
+    def device(where, which):
+        x, y, z = where
+        return (lax.rem(x, 2) * 2 + which, (y * RING + z) * 2 + x // 2)
+
+    def along(axis, d):
+        where = list(pos)
+        where[axis] = lax.rem(where[axis] + d, RING)
+        return device(where, core)
+
+    mate = device(pos, 1 - core)
+    blks = lax.axis_size("blk")
+    ahead = [(grp, lax.rem(blk + s, blks)) for s in range(1, VISITS)]
+    behind = [(grp, lax.rem(blk + blks - s, blks)) for s in range(1, VISITS)]
+    mates = [mate] + [along(axis, d) for axis in range(3) for d in range(1, RING)]
+
+    barrier = pltpu.get_barrier_semaphore()
+    for other in mates + behind:
+        pl.semaphore_signal(barrier, inc=1, device_id=other, device_id_type=MESH)
+    pl.semaphore_wait(barrier, len(mates) + len(ahead))
+
+    def remote(src, dst, send, recv, who):
+        return pltpu.make_async_remote_copy(
+            src_ref=src, dst_ref=dst, send_sem=send, recv_sem=recv, device_id=who, device_id_type=MESH
+        )
+
+    half = gram_ref.shape[0] // 2
+    third = half // PARTS
+    q1 = third // RING
+    q2 = q1 // RING
+
+    def rows(start, size):
+        return pl.ds(pl.multiple_of(start, 8), size)
+
+    c0, c1, c2, c3, c4, c5, c6, c7 = {}, {}, {}, {}, {}, {}, {}, {}
+    for p in range(PARTS):
+        c0[p] = remote(
+            gram_ref.at[rows((1 - core) * half + p * third, third)], pair.at[p], send0.at[p], recv0.at[p], mate
+        )
+        c0[p].start()
+    nt = target_ref.shape[0]
+    for s in range(1, VISITS):
+        c7[s] = remote(target_ref, right_ref.at[pl.ds(s * nt, nt)], send7.at[s - 1], recv7.at[s - 1], ahead[s - 1])
+        c7[s].start()
+    right_ref[0:nt, :] = target_ref[...]
+
+    steps = range(1, RING)
+    for p in range(PARTS):
+        axis = p
+        c0[p].wait_recv()
+        work[p] = gram_ref[rows(core * half + p * third, third), :] + pair[p]
+        for d in steps:
+            c1[p, d] = remote(
+                work.at[p, rows(lax.rem(pos[axis] + d, RING) * q1, q1)],
+                got1.at[p, d - 1], send1.at[p, d - 1], recv1.at[p, d - 1], along(axis, d),
+            )
+            c1[p, d].start()
+    for p in range(PARTS):
+        axis = (p + 1) % 3
+        for d in steps:
+            c1[p, d].wait_recv()
+        mine = work[p, rows(pos[p] * q1, q1), :]
+        sum1[p] = (mine + got1[p, 0]) + (got1[p, 1] + got1[p, 2])
+        for d in steps:
+            c2[p, d] = remote(
+                sum1.at[p, rows(lax.rem(pos[axis] + d, RING) * q2, q2)],
+                got2.at[p, d - 1], send2.at[p, d - 1], recv2.at[p, d - 1], along(axis, d),
+            )
+            c2[p, d].start()
+    for p in range(PARTS):
+        axis = (p + 2) % 3
+        for d in steps:
+            c2[p, d].wait_recv()
+        mine = sum1[p, rows(pos[(p + 1) % 3] * q2, q2), :]
+        sum2[p] = (mine + got2[p, 0]) + (got2[p, 1] + got2[p, 2])
+        for d in steps:
+            c3[p, d] = remote(sum2.at[p], got3.at[p, d - 1], send3.at[p, d - 1], recv3.at[p, d - 1], along(axis, d))
+            c3[p, d].start()
+    for p in range(PARTS):
+        axis = (p + 1) % 3
+        for d in steps:
+            c3[p, d].wait_recv()
+        spot = rows(pos[axis] * q2, q2)
+        full2[p, spot, :] = (sum2[p] + got3[p, 0]) + (got3[p, 1] + got3[p, 2])
+        for d in steps:
+            c4[p, d] = remote(
+                full2.at[p, spot], full2.at[p, spot], send4.at[p, d - 1], recv4.at[p, d - 1], along(axis, d)
+            )
+            c4[p, d].start()
+    own = []
+    for p in range(PARTS):
+        for d in steps:
+            c4[p, d].wait_recv()
+        spot = rows(core * half + p * third + pos[p] * q1, q1)
+        for d in steps:
+            c5[p, d] = remote(full2.at[p], out_ref.at[spot], send5.at[p, d - 1], recv5.at[p, d - 1], along(p, d))
+            c5[p, d].start()
+        c6[p, 0] = remote(full2.at[p], out_ref.at[spot], send6.at[p, 0], recv6.at[p, 0], mate)
+        c6[p, 0].start()
+        own.append(pltpu.make_async_copy(full2.at[p], out_ref.at[spot], own_sem.at[p]))
+        own[-1].start()
+    for d in (1, 3, 2):
+        for p in range(PARTS):
+            c5[p, d].wait_recv()
+            spot = rows(core * half + p * third + lax.rem(pos[p] + RING - d, RING) * q1, q1)
+            c6[p, d] = remote(out_ref.at[spot], out_ref.at[spot], send6.at[p, d], recv6.at[p, d], mate)
+            c6[p, d].start()
+    for copies in (c0, c1, c2, c3, c4, c5, c6, c7):
+        for copy in copies.values():
+            copy.wait_send()
+    for copy in own:
+        copy.wait()
+    for copies in (c6, c7):
+        for copy in copies.values():
+            copy.wait_recv()
+
+
+def summed_over_devices(gram, targets):
+    total_rows = gram.shape[0]
+    third = total_rows // (2 * PARTS)
+    q1, q2 = third // RING, third // (RING * RING)
+    sem = pltpu.SemaphoreType.DMA
+    fan = RING - 1
+    pairs = [(PARTS,)] + [(PARTS, fan)] * 5 + [(PARTS, RING), (VISITS - 1,)]
+    return pl.pallas_call(
+        sum_kernel,
+        out_shape=(
+            jax.ShapeDtypeStruct(gram.shape, F32),
+            jax.ShapeDtypeStruct((VISITS * targets.shape[0], targets.shape[1]), BF16),
+        ),
+        in_specs=[pl.BlockSpec(memory_space=pltpu.VMEM)] * 2,
+        out_specs=[pl.BlockSpec(memory_space=pltpu.VMEM)] * 2,
+        scratch_shapes=[
+            pltpu.VMEM((PARTS, third, NB), F32),
+            pltpu.VMEM((PARTS, third, NB), F32),
+            pltpu.VMEM((PARTS, fan, q1, NB), F32),
+            pltpu.VMEM((PARTS, q1, NB), F32),
+            pltpu.VMEM((PARTS, fan, q2, NB), F32),
+            pltpu.VMEM((PARTS, q2, NB), F32),
+            pltpu.VMEM((PARTS, fan, q2, NB), F32),
+            pltpu.VMEM((PARTS, q1, NB), F32),
+        ]
+        + [sem(shape) for shape in pairs for _ in range(2)]
+        + [sem((PARTS,))],
+        compiler_params=pltpu.CompilerParams(
+            collective_id=0, has_side_effects=True, vmem_limit_bytes=56 << 20
+        ),
+        name="summed_over_devices",
+    )(gram, targets)
 
 
 def per_device(train_grads, targets):
     rows_total = train_grads.shape[0] * lax.axis_size("grp") * lax.axis_size("blk")
-    visiting = [targets]
-    for step in range(1, VISITS):
-        visiting.append(passed_along(targets, "blk", step))
-    right = jnp.concatenate(visiting, axis=0)
-    local_gram = lax.dot_general(train_grads, train_grads, (((0,), (0,)), ((), ())), preferred_element_type=F32)
-    gram = lax.psum(local_gram, ("grp", "blk"))
+    gram, right = summed_over_devices(packed_gram(train_grads), targets)
     return solve_and_score(gram, right, train_grads, rows_total)
 
 

time: 248 us -> 118 us (0.48)
  waiting for transfers between devices: 152 us -> 0 us
  Pallas kernels: 60.3 us -> 118 us
  matrix products: 15.1 us -> 0 us
  between operations: 13.4 us -> 0.02 us
  starting transfers between devices: 5.21 us -> 0 us
    psum x1 -> x0, waiting for transfers between devices: 133 us -> none  [per_device(): gram = lax.psum(local_gram, ('grp', 'blk'))]
    pallas_call x0 -> x2, Pallas kernels: none -> 58.1 us  [the longest x1 49.1 us: summed_over_devices(): pl.pallas_call(sum_kernel, out_shape=(jax.ShapeDtypeStruct(gram.shape, F3...]
    ppermute x2 -> x0, waiting for transfers between devices: 18.6 us -> none  [passed_along(): return lax.ppermute(value, axis, pairs)]
    dot_general x1 -> x0, matrix products: 15.1 us -> none  [per_device(): lax.dot_general(train_grads, train_grads, (((0,), (0,)), ((), ())), prefe...]
    ppermute x2 -> x0, starting transfers between devices: 5.21 us -> none  [passed_along(): return lax.ppermute(value, axis, pairs)]
  transfers between devices with their start and end apart: 3 -> 0, of which waited for: 3 -> 0; matrix products, arithmetic and copies ran while one was open for 0% -> 0% of each run, Pallas kernels for 0% -> 0%
where the time goes in v2:
time: 118 us
  Pallas kernels  118 us (100%)
    pallas_call x1, Pallas kernels, solve_and_score(): pl.pallas_call(functools.partial(solve_kernel, rows_total), out_shape=jax...  60 us
    pallas_call x1, Pallas kernels, summed_over_devices(): pl.pallas_call(sum_kernel, out_shape=(jax.ShapeDtypeStruct(gram.shape, F3...  49.1 us
    pallas_call x1, Pallas kernels, packed_gram(): pl.pallas_call(gram_kernel, out_shape=jax.ShapeDtypeStruct((count * NB, N...  9.02 us

profile of v2, /device:TPU:1, one launch (start us, length us, event | category | flops | bytes accessed | tf_op | source)
XLA Modules:
  0.0 118.1 jit_solution(10074908555276377241)
XLA Ops:
  0.0 9.0 %packed_gram.1.gram_ref = f32[4608,128]{1,0:T(8,128)} custom-call(bf16[4096,1024]{1,0:T(8,128)(2,1)} %train_ref.3), custom_call_target="tpu_custom_call" | custom-call | tf_op jit(solution)/shard_map/packed_gram/pallas_call | solution.py:248
  9.0 49.1 %summed_over_devices.1 = (f32[4608,128]{1,0:T(8,128)}, bf16[384,1024]{1,0:T(8,128)(2,1)}) custom-call(f32[4608,128]{1,0:T(8,128)} %packed_gram.1.gram_ref, bf16[128,1024]{1,0:T(8,128)(2,1)} %target_ref.1), custom_call_target="tpu_custom_call" | custom-call | tf_op jit(solution)/shard_map/summed_over_devices/pallas_call | solution.py:394
  58.1 60.0 %solve_and_score.1 = bf16[4096,384]{1,0:T(8,128)(2,1)} custom-call(f32[4608,128]{1,0:T(8,128)} %get-tuple-element.7.gram_ref, bf16[384,1024]{1,0:T(8,128)(2,1)} %get-tuple-element.8.right_ref, bf16[4096,1024]{1,0:T(8,128)(2,1)} %train_ref.3), custom_call_target="tpu_custom_call" | custom-call | tf_op jit(solution)/shard_map/solve_and_score/pallas_call | solution.py:195
